TPU v7x, 32 devices: a whole 2x2x4 slice. The times are simulated.
32 devices in a mesh: lat: 8 (over z, y), lev: 4 (over x, core).
Axes of the slice: x: 2, y: 2, z: 4, core: 2. Of those that a mesh axis runs over, the one named last changes fastest.
Arguments:
- grid: bfloat16 [3, 1536, 32, 2816], P(None, 'lat', 'lev'), may hold values from -6 to 6
- legendre: bfloat16 [384, 769, 1280], P(('lat', 'lev')), may hold values from -6 to 6
- gauss_weights: float32 [1280], replicated, may hold values from 0.00078125 to 0.003125
- band_counts: int32 [8], replicated, may hold values from 1 to 192, 1280 in all
- pair_m: int32 [384], replicated, may hold values from 0 to 383, each once
- vert_modes: float32 [32, 32], replicated, may hold values from -1 to 1
- mode_depth: float32 [32], replicated, may hold values from 0.5 to 50
- diffusion: float32 [32], replicated, may hold values from 1 to 100
- pressure_balance_matrix: float32 [32, 32], replicated, may hold values from -1 to 1
Outputs:
- next_grid_rows: bfloat16 [3, 1536, 32, 2816], P(None, 'lat', 'lev')
Inputs may be any that keep to these rules, and one draw needn't show every extreme that they name: `band_counts`: latitudes in each band, in band order; the bands cover all 1280 latitudes and the fullest holds 192. `pair_m`: each of 0 to 383 once.
All inputs are finite; a program needn't handle non-finite values.
Results may differ from a plain program's by a relative error of at most 0.0072.
Values may be sent and summed in bfloat16 or wider, within the bound.
No kernel may reach another device: no remote copies, remote signals or barrier semaphores. Data moves between devices by JAX's collectives and lax.ppermute only.
A program may use at most 576 MiB of HBM per device.

v0:
```python
import math

import jax
import jax.numpy as jnp
from jax import lax
from jax.sharding import PartitionSpec as P


def dft_tables(pair_m, width, points):
    upper_wave = width - 1 - pair_m
    harmonic_order_index = jnp.stack([pair_m, pair_m, upper_wave, upper_wave], axis=1).reshape(-1)
    component = jnp.arange(2 * width, dtype=jnp.int32) % 2
    phase_index = (
        harmonic_order_index[:, None] * jnp.arange(points, dtype=jnp.int32)[None, :] % points
    )
    angles = phase_index.astype(jnp.float32) * (2.0 * math.pi / points)
    trig_values = jnp.where((component == 0)[:, None], jnp.cos(angles), -jnp.sin(angles))
    factor = jnp.where(harmonic_order_index == 0, 1.0, 2.0).astype(jnp.float32)
    forward_table = (trig_values / points).astype(jnp.bfloat16)
    inverse_table = (trig_values * factor[:, None]).astype(jnp.bfloat16)
    return (forward_table, inverse_table)


def latitude_maps(band_counts, lat_cap):
    group_count = band_counts.shape[0]
    band_starts = jnp.cumsum(band_counts) - band_counts
    groups = jnp.arange(group_count, dtype=jnp.int32)
    slot_ids = jnp.arange(group_count * lat_cap, dtype=jnp.int32)
    slot_band = slot_ids // lat_cap
    offsets = slot_ids % lat_cap
    member = groups[None, :] == slot_band[:, None]
    slot_begin = jnp.sum(jnp.where(member, band_starts[None, :], 0), axis=1)
    slot_size = jnp.sum(jnp.where(member, band_counts[None, :], 0), axis=1)
    valid_slot = offsets < slot_size
    lat_of_slot = jnp.where(valid_slot, slot_begin + offsets, 0)
    return (lat_of_slot, valid_slot, band_starts)


def helmholtz(
    harmonic_model_snapshot, ratio, vert_modes, mode_depth, diffusion, pressure_balance_matrix
):
    rotation_harmonic_coeffs = harmonic_model_snapshot[..., 0, :, :]
    velocity_spread_coeffs_map = harmonic_model_snapshot[..., 1, :, :]
    thermal_harmonic_coeffs = harmonic_model_snapshot[..., 2, :, :]
    rotation_harmonic_coeffs = rotation_harmonic_coeffs / (1.0 + diffusion[:, None] * ratio * ratio)
    modes = jnp.einsum(
        "ql,...lk->...qk", vert_modes, velocity_spread_coeffs_map, precision=lax.Precision.HIGHEST
    )
    modes = modes / (1.0 + mode_depth[:, None] * ratio)
    velocity_spread_coeffs_map = jnp.einsum(
        "ql,...qk->...lk", vert_modes, modes, precision=lax.Precision.HIGHEST
    )
    thermal_harmonic_coeffs = thermal_harmonic_coeffs - jnp.einsum(
        "ja,...ax->...jx",
        pressure_balance_matrix,
        velocity_spread_coeffs_map,
        precision=lax.Precision.HIGHEST,
    )
    return jnp.stack(
        [rotation_harmonic_coeffs, velocity_spread_coeffs_map, thermal_harmonic_coeffs], axis=-3
    )


def shards(
    grid,
    legendre,
    gauss_weights,
    band_counts,
    pair_m,
    vert_modes,
    mode_depth,
    diffusion,
    pressure_balance_matrix,
):
    lat_groups = lax.axis_size("lat")
    lev_groups = lax.axis_size("lev")
    device_count = lat_groups * lev_groups
    fields, lat_cap, lev_dev, points = grid.shape
    pair_dev, row_count, lat_total = legendre.shape
    width = row_count - 1
    half_rows = width // 2 + 1
    level_total = lev_dev * lev_groups
    my_band = lax.axis_index("lat")
    owner_index = my_band * lev_groups + lax.axis_index("lev")
    lat_of_slot, valid_slot, band_starts = latitude_maps(band_counts, lat_cap)
    band_match = jnp.arange(lat_groups, dtype=jnp.int32) == my_band
    my_start = jnp.sum(jnp.where(band_match, band_starts, 0))
    my_count = jnp.sum(jnp.where(band_match, band_counts, 0))
    row_valid = jnp.arange(lat_cap, dtype=jnp.int32) < my_count
    padded_weights = jnp.concatenate([gauss_weights, jnp.zeros((lat_cap,), jnp.float32)])
    row_weights = jnp.where(
        row_valid, lax.dynamic_slice(padded_weights, (my_start,), (lat_cap,)), 0.0
    )
    forward_table, inverse_table = dft_tables(pair_m, width, points)
    coeffs = lax.dot_general(
        forward_table, grid, (((1,), (3,)), ((), ())), preferred_element_type=jnp.float32
    )
    coeffs = (coeffs * row_weights[None, None, :, None]).astype(jnp.bfloat16)
    coeffs = coeffs.reshape(device_count, pair_dev * 4, fields, lat_cap * lev_dev)
    slot_table = jnp.take(legendre, lat_of_slot, axis=2) * valid_slot.astype(jnp.bfloat16)
    slot_table = slot_table.reshape(pair_dev, row_count, lat_groups, lat_cap)
    table_head = slot_table[:, :half_rows]
    table_tail = slot_table[:, half_rows:]
    local_waves = lax.dynamic_slice(pair_m, (owner_index * pair_dev,), (pair_dev,))
    row_ids = jnp.arange(row_count, dtype=jnp.int32)
    own_rows = row_ids[None, :] < (width - local_waves)[:, None]
    degree = jnp.where(own_rows, local_waves[:, None] + row_ids[None, :], row_ids[None, :] - 1)
    ratio = (degree * (degree + 1)).astype(jnp.float32) / float(width * (width - 1))
    tail_own = own_rows[:, half_rows:]
    received = lax.all_to_all(coeffs, ("lat", "lev"), split_axis=0, concat_axis=0, tiled=True)
    field_part = received.shape[2]
    arranged = received.reshape(
        lat_groups, lev_groups, pair_dev, 2, 2, field_part, lat_cap, lev_dev
    )
    head_spec = jnp.einsum(
        "pkgs,glpcfsd->pcfldk", table_head, arranged[:, :, :, 0], preferred_element_type=jnp.float32
    )
    tail_both = jnp.einsum(
        "pkgs,glpwcfsd->pwcfldk", table_tail, arranged, preferred_element_type=jnp.float32
    )
    tail_spec = jnp.where(tail_own[:, None, None, None, None, :], tail_both[:, 0], tail_both[:, 1])
    harmonic_model_snapshot = jnp.concatenate([head_spec, tail_spec], axis=-1)
    harmonic_space_module = harmonic_model_snapshot.reshape(
        pair_dev, 2, field_part, level_total, row_count
    )
    updated = helmholtz(
        harmonic_space_module,
        ratio[:, None, None, :],
        vert_modes,
        mode_depth,
        diffusion,
        pressure_balance_matrix,
    ).astype(jnp.bfloat16)
    updated = updated.reshape(pair_dev, 2, fields, lev_groups, lev_dev, row_count)
    head_part = jnp.einsum(
        "pkgs,prfldk->glprfsd",
        table_head,
        updated[..., :half_rows],
        preferred_element_type=jnp.float32,
    )
    masks = jnp.stack([tail_own, jnp.logical_not(tail_own)], axis=1).astype(jnp.bfloat16)
    masked = updated[:, None, ..., half_rows:] * masks[:, :, None, None, None, None, :]
    tail_parts = jnp.einsum(
        "pkgs,pwrfldk->glpwrfsd", table_tail, masked, preferred_element_type=jnp.float32
    )
    synthesis = jnp.stack(
        [tail_parts[:, :, :, 0] + head_part, tail_parts[:, :, :, 1]], axis=3
    ).astype(jnp.bfloat16)
    banded = synthesis.reshape(device_count, pair_dev * 4, fields, lat_cap * lev_dev)
    received = lax.all_to_all(banded, ("lat", "lev"), split_axis=0, concat_axis=0, tiled=True)
    field_part = received.shape[2]
    columns = received.reshape(2 * width, field_part, lat_cap * lev_dev)
    values = lax.dot_general(
        columns, inverse_table, (((0,), (0,)), ((), ())), preferred_element_type=jnp.float32
    )
    return values.reshape(field_part, lat_cap, lev_dev, points).astype(jnp.bfloat16)


def solution(mesh):
    placed = (
        P(None, "lat", "lev", None),
        P(("lat", "lev"), None, None),
        P(),
        P(),
        P(),
        P(),
        P(),
        P(),
        P(),
    )
    return jax.shard_map(
        shards, mesh=mesh, in_specs=placed, out_specs=P(None, "lat", "lev", None), check_vma=False
    )
```

profile of v0, /device:TPU:0, one launch (start us, length us, event | category | flops | bytes accessed | tf_op | source)
XLA Modules:
  0.0 2052.8 jit_solution(3533842021564197527)
XLA Ops:
  5.8 76.0 %fusion.111 = bf16[1536,2816,1,1]{1,0,3,2:T(8,128)(2,1)} fusion(s32[1536]{0:T(1024)S(1)} %mul.117, pred[1536]{0:T(1024)(128)(4,1)S(1)} %fusion.77), kind=kLoop, calls=%fused_computation.35.clone.clone.1 | loop fusion | flops 56229888 | bytes 8658432 | tf_op jit(solution)/shard_map/dot_general | solution.py:95
  82.5 46.2 %multiply_convert_fusion = bf16[1536,3,192,8]{0,2,3,1:T(8,128)(2,1)S(1)} fusion(bf16[3,192,8,2816]{3,2,1,0:T(8,128)(2,1)} %param.9, f32[192]{0:T(256)S(1)} %compare_select_fusion.4, bf16[1536,2816,1,1]{1,0,3,2:T(8,128)(2,1)} %fusion.111), kind=kOutput, calls=%fused_computation.4 | convolution fusion | flops 39876820992 | bytes 48759552 | tf_op jit(solution)/shard_map/dot_general | solution.py:95
  128.7 18.3 copy.125
  147.0 48.3 %reshape.253 = bf16[32,48,3,1536]{1,0,3,2:T(8,128)(2,1)} reshape(bf16[1536,3,192,8]{0,3,2,1:T(8,128)(2,1)} %copy.125) | data formatting | bytes 28311552 | tf_op jit(solution)/shard_map/reshape | solution.py:99
  195.3 38.8 %copy.126 = bf16[32,48,3,1536]{3,1,2,0:T(8,128)(2,1)} copy(bf16[32,48,3,1536]{1,0,3,2:T(8,128)(2,1)} %reshape.253) | data formatting | bytes 28311552 | tf_op jit(solution)/shard_map/reshape | solution.py:99
  242.0 49.1 %copy.128 = bf16[12,769,1280]{1,0,2:T(8,128)(2,1)} copy(bf16[12,769,1280]{2,1,0:T(8,128)(2,1)} %param.10) | data formatting | bytes 47247360 | tf_op args[1]
  291.1 44.9 %gather_fusion = bf16[1536,12,769]{2,1,0:T(8,128)(2,1)} fusion(bf16[12,769,1280]{1,0,2:T(8,128)(2,1)} %copy.128, s32[2048]{0:T(1024)S(1)} %pad_clamp_fusion), kind=kCustom, calls=%fused_computation | custom fusion | bytes 56702976 | tf_op jit(solution)/shard_map/jit(_take)/gather | solution.py:100
  336.0 26.3 %copy.129 = bf16[12,769,1536]{1,2,0:T(8,128)(2,1)} copy(bf16[12,769,1536]{1,0,2:T(8,128)(2,1)} %bitcast.180) | data formatting | bytes 56696832 | tf_op jit(solution)/shard_map/jit(_take)/gather | solution.py:100
  366.7 22.8 %select_multiply_fusion = bf16[12,769,8,192]{1,3,2,0:T(8,128)(2,1)} fusion(bf16[12,769,8,192]{1,3,2,0:T(8,128)(2,1)} %bitcast.179, pred[8,192]{1,0:T(8,128)(4,1)S(1)} %compare_and_fusion, bf16[8,192]{1,0:T(8,128)(2,1)S(1)} %get-tuple-element.11), kind=kLoop, calls=%fused_computation.3 | loop fusion | flops 28348416 | bytes 56701440 | tf_op jit(solution)/shard_map/mul | solution.py:100
  389.5 166.2 %all-to-all-done = bf16[32,48,3,1536]{3,1,2,0:T(8,128)(2,1)} async-done(((bf16[32,48,3,1536]{3,1,2,0:T(8,128)(2,1)}), bf16[32,48,3,1536]{3,1,2,0:T(8,128)(2,1)}, u32[]{:S(2)}, u32[]{:S(2)}) %all-to-all-start) | async-done | bytes 14155808 | tf_op jit(solution)/shard_map/all_to_all | solution.py:110
  555.7 272.4 %reshape.254 = bf16[8,4,12,2,2,3,192,8]{7,6,4,3,2,5,1,0:T(8,128)(2,1)} reshape(bf16[32,48,3,1536]{3,1,2,0:T(8,128)(2,1)} %all-to-all-done) | data formatting | bytes 28311552 | tf_op jit(solution)/shard_map/reshape | solution.py:112
  828.2 73.7 %slice.55 = bf16[8,4,12,1,2,3,192,8]{7,6,4,3,2,5,1,0:T(8,128)(2,1)} slice(bf16[8,4,12,2,2,3,192,8]{7,6,4,3,2,5,1,0:T(8,128)(2,1)} %reshape.254), slice={[0:8], [0:4], [0:12], [0:1], [0:2], [0:3], [0:192], [0:8]} | slice | bytes 14155776 | tf_op jit(solution)/shard_map/slice | solution.py:116
  901.9 86.4 %fusion.44 = f32[12,4,2,2,3,8,384]{6,5,2,4,3,1,0:T(8,128)} fusion(bf16[8,4,12,2,2,3,192,8]{7,6,4,3,2,5,1,0:T(8,128)(2,1)} %reshape.254, bf16[12,769,8,192]{1,3,2,0:T(8,128)(2,1)} %select_multiply_fusion), kind=kOutput, calls=%fused_computation.57 | convolution fusion | flops 5435817984 | bytes 247726080 | tf_op jit(solution)/shard_map/pkgs,glpwcfsd->pwcfldk/dot_general | solution.py:118
  995.1 89.6 %copy.164 = bf16[8,4,12,1,2,3,192,8]{6,7,0,5,4,1,2,3:T(8,128)(2,1)} copy(bf16[8,4,12,1,2,3,192,8]{7,6,4,3,2,5,1,0:T(8,128)(2,1)} %slice.55) | data formatting | bytes 14155776
  1084.7 11.2 fusion.59
  1113.5 26.6 %fusion.19 = f32[8,4,12,2,2,3,192,8]{6,7,0,1,5,4,3,2:T(8,128)} fusion(bf16[12,769,8,192]{1,3,2,0:T(8,128)(2,1)} %select_multiply_fusion, bf16[12,2,384]{2,1,0:T(2,128)(2,1)S(1)} %copy-done.5, bf16[12,2,3,4,8,384]{5,4,3,2,1,0:T(8,128)(2,1)} %pad_maximum_fusion.5), kind=kOutput, calls=%fused_computation.30 | convolution fusion | flops 5442895872 | bytes 44255232 | tf_op jit(solution)/shard_map/pkgs,pwrfldk->glpwrfsd/dot_general | solution.py:143
  1140.1 17.8 fusion.23
  1175.6 157.3 %copy.142 = bf16[8,4,12,2,2,3,192,8]{7,6,4,3,2,5,1,0:T(8,128)(2,1)} copy(bf16[8,4,12,2,2,3,192,8]{6,7,0,1,5,4,3,2:T(8,128)(2,1)} %pad_maximum_fusion) | data formatting | bytes 28311552 | tf_op jit(solution)/shard_map/stack | solution.py:146
  1332.9 324.5 %convert_element_type.49 = bf16[32,48,3,1536]{3,1,2,0:T(8,128)(2,1)} reshape(bf16[8,4,12,2,2,3,192,8]{7,6,4,3,2,5,1,0:T(8,128)(2,1)} %copy.142) | data formatting | bytes 28311552 | tf_op jit(solution)/shard_map/convert_element_type | solution.py:148
  1661.7 76.2 %fusion.113 = bf16[1536,2816,1,1]{1,0,3,2:T(8,128)(2,1)} fusion(f32[1536]{0:T(1024)S(1)} %compare_select_fusion.3, s32[1536]{0:T(1024)S(1)} %copy-done.7, pred[1536]{0:T(1024)(128)(4,1)S(1)} %copy-done.12), kind=kLoop, calls=%fused_computation.36.clone.clone.1 | loop fusion | flops 56229888 | bytes 8664576 | tf_op jit(solution)/shard_map/dot_general | solution.py:153
  1737.9 237.8 %all-to-all-done.1 = bf16[32,48,3,1536]{3,1,2,0:T(8,128)(2,1)} async-done(((bf16[32,48,3,1536]{3,1,2,0:T(8,128)(2,1)}), bf16[32,48,3,1536]{3,1,2,0:T(8,128)(2,1)}, u32[]{:S(2)}, u32[]{:S(2)}) %all-to-all-start.1) | async-done | bytes 14155808 | tf_op jit(solution)/shard_map/all_to_all | solution.py:150
  1975.8 10.5 copy.143
  1986.3 18.6 copy.144
  2004.9 47.4 %convolution_convert_fusion = bf16[3,192,8,2816]{3,2,1,0:T(8,128)(2,1)} fusion(bf16[3,1536,1536]{2,1,0:T(8,128)(2,1)} %copy.144, bf16[1536,2816,1,1]{1,0,3,2:T(8,128)(2,1)} %fusion.113), kind=kOutput, calls=%fused_computation.8 | convolution fusion | flops 39875641344 | bytes 48758784 | tf_op jit(solution)/shard_map/dot_general | solution.py:153
  (73 shorter events, 62.9 us)
Async XLA Ops:
  0.0 1101.6 %copy-start = (f32[32,32]{1,0:T(8,128)S(1)}, f32[32,32]{1,0:T(8,128)}, u32[]{:S(2)}) copy-start(f32[32,32]{1,0:T(8,128)} %param.14) | copy-start | bytes 12292
  0.0 81.8 %copy-start.10 = (f32[1280]{0:T(1024)S(1)}, f32[1280]{0:T(1024)}, u32[]{:S(2)}) copy-start(f32[1280]{0:T(1024)} %param.11) | copy-start | bytes 15364
  1.4 127.3 %copy-start.11 = (pred[1536]{0:T(1024)(128)(4,1)}, pred[1536]{0:T(1024)(128)(4,1)S(1)}, u32[]{:S(2)}) copy-start(pred[1536]{0:T(1024)(128)(4,1)S(1)} %fusion.77) | copy-start | bytes 4612
  5.2 123.5 %copy-start.6 = (s32[1536]{0:T(1024)}, s32[1536]{0:T(1024)S(1)}, u32[]{:S(2)}) copy-start(s32[1536]{0:T(1024)S(1)} %mul.117) | copy-start | bytes 18436
  234.1 7.7 copy-start.13
  234.1 321.7 %all-to-all-start = ((bf16[32,48,3,1536]{3,1,2,0:T(8,128)(2,1)}), bf16[32,48,3,1536]{3,1,2,0:T(8,128)(2,1)}, u32[]{:S(2)}, u32[]{:S(2)}) async-start(bf16[32,48,3,1536]{3,1,2,0:T(8,128)(2,1)} %copy.126), calls=%async_computation | async-start | bytes 28311552 | tf_op jit(solution)/shard_map/all_to_all | solution.py:110
  336.0 28.7 %copy-start.14 = (f32[32]{0:T(128)S(1)}, f32[32]{0:T(128)}, u32[]{:S(2)}) copy-start(f32[32]{0:T(128)} %param.16) | copy-start | bytes 388
  336.0 28.7 %copy-start.15 = (f32[32]{0:T(128)S(1)}, f32[32]{0:T(128)}, u32[]{:S(2)}) copy-start(f32[32]{0:T(128)} %param.15) | copy-start | bytes 388
  1084.7 11.2 copy-start.8
  1099.5 4.7 copy-start.4
  1101.6 5.5 copy-start.9
  1104.2 5.7 copy-start.3
  1107.1 6.4 copy-start.5
  1110.3 1.1 copy-start.2
  1157.9 9.1 copy-start.1
  1657.5 4.2 copy-start.7
  1657.5 4.2 copy-start.12
  1657.5 318.3 %all-to-all-start.1 = ((bf16[32,48,3,1536]{3,1,2,0:T(8,128)(2,1)}), bf16[32,48,3,1536]{3,1,2,0:T(8,128)(2,1)}, u32[]{:S(2)}, u32[]{:S(2)}) async-start(bf16[32,48,3,1536]{3,1,2,0:T(8,128)(2,1)} %convert_element_type.49), calls=%async_computation.1 | async-start | bytes 28311552 | tf_op jit(solution)/shard_map/all_to_all | solution.py:150
where the time goes:
time: 2070 us; the launch traced here: 2050 us
  local copies, waits for them, and re-layouts  1190 us (57%)
  waiting for transfers between devices  404 us (20%)
  matrix products  244 us (12%)
  other arithmetic  200 us (10%)
    convert_element_type x1, local copies, waits for them, and re-layouts, shards(): synthesis = jnp.stack([tail_parts[:, :, :, 0] + head_part, tail_parts[:,...  325 us
    reshape x1, local copies, waits for them, and re-layouts, shards(): received.reshape(lat_groups, lev_groups, pair_dev, 2, 2, field_part, lat_...  272 us
    all_to_all x1, waiting for transfers between devices, shards(): lax.all_to_all(banded, ('lat', 'lev'), split_axis=0, concat_axis=0, tiled...  238 us
    all_to_all x1, waiting for transfers between devices, shards(): lax.all_to_all(coeffs, ('lat', 'lev'), split_axis=0, concat_axis=0, tiled...  166 us
    another operation x1, local copies, waits for them, and re-layouts, shards(): jnp.stack([tail_parts[:, :, :, 0] + head_part, tail_parts[:, :, :, 1]], a...  157 us
    unnamed x34, local copies, waits for them, and re-layouts  142 us
    reshape x2, local copies, waits for them, and re-layouts, shards(): coeffs.reshape(device_count, pair_dev * 4, fields, lat_cap * lev_dev)  87 us
    dot_general x1, matrix products, shards(): jnp.einsum('pkgs,glpwcfsd->pwcfldk', table_tail, arranged, preferred_elem...  86.4 us
  transfers between devices with their start and end apart: 2, of which 2 were waited for; matrix products, arithmetic and copies ran while one was open for 11% of the time, Pallas kernels for 0%

commit v1 on v0

v1 whole, which is shorter than its diff:
```python
import functools
import math

import jax
import jax.numpy as jnp
from jax import lax
from jax.experimental import pallas as pl
from jax.experimental.pallas import tpu as pltpu
from jax.sharding import PartitionSpec as P

LANES = 128
VMEM_LIMIT = 56 * 1024 * 1024


def swap_units(parts, unit):
    lane = lax.broadcasted_iota(jnp.int32, parts[0].shape, 1)
    step = 1
    parts = list(parts)
    while step < len(parts):
        shift = unit * step
        high = (lane & shift) != 0
        for i in range(len(parts)):
            if not i & step:
                a, b = parts[i], parts[i | step]
                parts[i] = jnp.where(high, pltpu.roll(b, shift, 1), a)
                parts[i | step] = jnp.where(high, b, pltpu.roll(a, LANES - shift, 1))
        step *= 2
    return parts


def row_tile(rows, most):
    tile = most
    while rows % tile:
        tile -= 16
    return tile


def table_kernel(coarse_cos, coarse_sin, fine_cos, fine_sin, table):
    cos_b, sin_b = fine_cos[...], fine_sin[...]
    for a in range(table.shape[1] // LANES):
        values = coarse_cos[:, a : a + 1] * cos_b - coarse_sin[:, a : a + 1] * sin_b
        table[:, a * LANES : (a + 1) * LANES] = values.astype(table.dtype)


def trig_table(pair_m, width, points, devices, groups, group):
    pair_dev = pair_m.shape[0] // devices
    padded = jnp.pad(
        pair_m.reshape(devices, pair_dev),
        ((0, 0), (0, groups * group - pair_dev)),
        constant_values=-1,
    ).reshape(-1)
    waves = jnp.stack([padded, padded, width - 1 - padded, width - 1 - padded], axis=1).reshape(-1)
    real = jnp.repeat(padded >= 0, 4)
    rows = waves.shape[0]
    sine = (jnp.arange(rows, dtype=jnp.int32) % 2 == 1)[:, None]
    blocks = points // LANES
    unit = 2.0 * math.pi / points
    fine = (waves[:, None] * jnp.arange(LANES, dtype=jnp.int32)[None, :]) % points
    fine = fine.astype(jnp.float32) * unit
    coarse = (waves[:, None] * (LANES * jnp.arange(LANES, dtype=jnp.int32)[None, :])) % points
    coarse = coarse.astype(jnp.float32) * unit
    keep = real[:, None].astype(jnp.float32)
    cos_a, sin_a = jnp.cos(coarse) * keep, jnp.sin(coarse) * keep
    tile = row_tile(rows, 256) if rows % 256 == 0 else LANES
    narrow = pl.BlockSpec((tile, LANES), lambda t: (t, 0))
    return pl.pallas_call(
        table_kernel,
        grid=(rows // tile,),
        in_specs=[narrow] * 4,
        out_specs=pl.BlockSpec((tile, points), lambda t: (t, 0)),
        out_shape=jax.ShapeDtypeStruct((rows, points), jnp.bfloat16),
        cost_estimate=pl.CostEstimate(
            flops=4 * rows * points, bytes_accessed=2 * rows * points, transcendentals=0
        ),
        name="trig_table",
    )(
        jnp.where(sine, -sin_a, cos_a),
        jnp.where(sine, cos_a, sin_a),
        jnp.cos(fine),
        jnp.sin(fine),
    )


def forward_kernel(levels, unit, grid_ref, table_ref, weight_ref, out_ref, scratch):
    cols = table_ref.shape[0]
    rows = grid_ref.shape[1]
    cap = rows // levels
    tile = row_tile(cap, 32)
    for r in range(cap // tile):
        lo = r * tile * levels
        values = lax.dot_general(
            grid_ref[0, lo : lo + tile * levels, :],
            table_ref[...],
            (((1,), (1,)), ((), ())),
            preferred_element_type=jnp.float32,
        )
        for n in range(cols // LANES):
            scratch[n, lo : lo + tile * levels, :] = values[:, n * LANES : (n + 1) * LANES]
        weight = weight_ref[r * tile : (r + 1) * tile, :]
        for n in range(cols // LANES):
            parts = [
                scratch[n, pl.ds(lo + l, tile, stride=levels), :] * weight for l in range(levels)
            ]
            for a, part in enumerate(swap_units(parts, unit)):
                out_ref[n * levels + a, r * tile : (r + 1) * tile, :] = part.astype(jnp.bfloat16)


def forward(field, grid, table, weights, levels, unit):
    _, rows, points = grid.shape
    columns = table.shape[0]
    cap = rows // levels
    step = 2 * LANES if columns % (2 * LANES) == 0 else LANES
    pieces = step // unit
    return pl.pallas_call(
        functools.partial(forward_kernel, levels, unit),
        grid=(columns // step,),
        in_specs=[
            pl.BlockSpec((1, rows, points), lambda t: (field, 0, 0)),
            pl.BlockSpec((step, points), lambda t: (t, 0)),
            pl.BlockSpec((cap, LANES), lambda t: (0, 0)),
        ],
        out_specs=pl.BlockSpec((pieces, cap, LANES), lambda t: (t, 0, 0)),
        out_shape=jax.ShapeDtypeStruct((columns // unit, cap, LANES), jnp.bfloat16),
        scratch_shapes=[pltpu.VMEM((step // LANES, rows, LANES), jnp.float32)],
        compiler_params=pltpu.CompilerParams(vmem_limit_bytes=VMEM_LIMIT),
        cost_estimate=pl.CostEstimate(
            flops=2 * rows * points * columns,
            bytes_accessed=2 * (rows * points + columns * points + rows * columns),
            transcendentals=0,
        ),
        name="forward_dft",
    )(grid, table, weights)


def inverse_kernel(levels, unit, count_ref, spec_ref, table_ref, *rest):
    out_ref, scratch = rest[-2:]
    pieces, tile, _ = spec_ref.shape
    for n in range(pieces // levels):
        parts = [spec_ref[n * levels + a].astype(jnp.float32) for a in range(levels)]
        for l, part in enumerate(swap_units(parts, unit)):
            scratch[n, pl.ds(l, tile, stride=levels), :] = part
    rows = tile * levels
    row = pl.program_id(0) * rows + lax.broadcasted_iota(jnp.int32, (rows, LANES), 0)
    valid = row < count_ref[0] * levels
    columns = jnp.concatenate(
        [
            jnp.where(valid, scratch[n], 0.0).astype(jnp.bfloat16)
            for n in range(pieces // levels)
        ],
        axis=1,
    )
    out_ref[0] = jnp.dot(columns, table_ref[...], preferred_element_type=jnp.float32).astype(
        out_ref.dtype
    )


def inverse(field, fields, spec, table, count, partial, levels, unit):
    pieces, cap, _ = spec.shape
    columns, points = table.shape
    rows = cap * levels
    tile = row_tile(cap, 32)
    in_specs = [
        pl.BlockSpec((pieces, tile, LANES), lambda t, c: (0, t, 0)),
        pl.BlockSpec((columns, points), lambda t, c: (0, 0)),
    ]
    operands = [spec, table]
    if partial is not None:
        in_specs.append(pl.BlockSpec(memory_space=pl.ANY))
        operands.append(partial)
    return pl.pallas_call(
        functools.partial(inverse_kernel, levels, unit),
        grid_spec=pltpu.PrefetchScalarGridSpec(
            num_scalar_prefetch=1,
            grid=(cap // tile,),
            in_specs=in_specs,
            out_specs=pl.BlockSpec((1, tile * levels, points), lambda t, c: (field, t, 0)),
            scratch_shapes=[pltpu.VMEM((pieces // levels, tile * levels, LANES), jnp.float32)],
        ),
        out_shape=jax.ShapeDtypeStruct((fields, rows, points), jnp.bfloat16),
        input_output_aliases={} if partial is None else {3: 0},
        compiler_params=pltpu.CompilerParams(vmem_limit_bytes=VMEM_LIMIT),
        cost_estimate=pl.CostEstimate(
            flops=2 * rows * points * columns,
            bytes_accessed=2 * (rows * points + columns * points + rows * columns),
            transcendentals=0,
        ),
        name="inverse_dft",
    )(count, *operands)


def legendre_kernel(
    kind, pair_dev, lat_groups, group, counts_ref, waves_ref, recv_ref, leg_ref, *rest
):
    lane_ref = rest[0]
    if kind == "vorticity":
        out_ref, gathered, made = rest[1:]
    elif kind == "divergence":
        to_modes, from_modes, out_ref, div_out, gathered, made = rest[1:]
    else:
        balance, div_in, out_ref, gathered, made = rest[1:]
    row_count, lat_total = leg_ref.shape[1:]
    width = row_count - 1
    cap = recv_ref.shape[2]
    member = pl.program_id(1)
    pair = pl.program_id(0) * group + member

    @pl.when(member == 0)
    def _():
        start = 0
        for g in range(lat_groups):
            parts = [recv_ref[g * group + h, 0].astype(jnp.float32) for h in range(group)]
            for b, part in enumerate(swap_units(parts, 4)):
                gathered[b, pl.ds(start, cap), :] = part
            start = start + counts_ref[g]

    @pl.when(pair < pair_dev)
    def _():
        wave = waves_ref[pair]
        coeffs = gathered[member, :lat_total, :].astype(jnp.bfloat16)
        main = leg_ref[0, :width, :]
        last = jnp.broadcast_to(leg_ref[0, width:, :], (16, lat_total))
        spectral = jnp.concatenate(
            [
                jnp.dot(main, coeffs, preferred_element_type=jnp.float32),
                jnp.dot(last, coeffs, preferred_element_type=jnp.float32),
            ],
            axis=0,
        )
        shape = spectral.shape
        row = lax.broadcasted_iota(jnp.int32, shape, 0)
        lane = lax.broadcasted_iota(jnp.int32, shape, 1)
        own = row < width - wave
        upper = (lane & 2) != 0
        keep = jnp.logical_and(jnp.logical_xor(own, upper), row < row_count)
        degree = jnp.where(own, row + wave, row - 1)
        ratio = (degree * (degree + 1)).astype(jnp.float32) / float(width * (width - 1))
        spectral = jnp.where(keep, spectral, 0.0)
        exact = functools.partial(
            jnp.dot, precision=lax.Precision.HIGHEST, preferred_element_type=jnp.float32
        )
        if kind == "vorticity":
            new = spectral / (1.0 + lane_ref[...] * ratio * ratio)
        elif kind == "divergence":
            modes = exact(spectral, to_modes[...])
            modes = modes / (1.0 + lane_ref[...] * ratio)
            new = exact(modes, from_modes[...])
            div_out[0] = new
        else:
            new = spectral - exact(div_in[0], balance[...])
        zonal = jnp.logical_and(wave == 0, jnp.logical_not(upper))
        new = new * jnp.where(zonal, 1.0, 2.0)
        tail = jnp.concatenate(
            [new[width:], jnp.zeros((LANES - 16, LANES), jnp.float32)], axis=0
        )
        turned = jnp.dot(
            new[:width].T.astype(jnp.bfloat16), main, preferred_element_type=jnp.float32
        )
        turned += jnp.dot(
            tail.T.astype(jnp.bfloat16),
            jnp.broadcast_to(leg_ref[0, width:, :], (LANES, lat_total)),
            preferred_element_type=jnp.float32,
        )
        made[member, :lat_total, :] = turned.T
        made[member, lat_total:, :] = jnp.zeros((cap, LANES), jnp.float32)

    @pl.when(pair >= pair_dev)
    def _():
        made[member] = jnp.zeros(made.shape[1:], jnp.float32)

    @pl.when(member == group - 1)
    def _():
        start = 0
        for g in range(lat_groups):
            parts = [made[b, pl.ds(start, cap), :] for b in range(group)]
            for h, part in enumerate(swap_units(parts, 4)):
                out_ref[g * group + h, 0] = part.astype(jnp.bfloat16)
            start = start + counts_ref[g]


def legendre_step(kind, received, legendre, counts, waves, lane_values, extra, group):
    devices, groups, cap, _ = received.shape
    pair_dev, row_count, lat_total = legendre.shape
    lat_groups = devices // group

    def at_pair(i, b, *_):
        return (jnp.minimum(i * group + b, pair_dev - 1), 0, 0)

    def whole(i, b, *_):
        return (0, 0)

    blocks = pl.BlockSpec((devices, 1, cap, LANES), lambda i, b, *_: (0, i, 0, 0))
    square = pl.BlockSpec((LANES, LANES), whole)
    div_block = pl.BlockSpec((1, row_count + 15, LANES), at_pair)
    in_specs = [
        blocks,
        pl.BlockSpec((1, row_count, lat_total), at_pair),
        pl.BlockSpec((1, LANES), whole),
    ]
    out_specs = [blocks]
    out_shape = [jax.ShapeDtypeStruct(received.shape, jnp.bfloat16)]
    if kind == "divergence":
        in_specs += [square, square]
        out_specs.append(div_block)
        out_shape.append(jax.ShapeDtypeStruct((pair_dev, row_count + 15, LANES), jnp.float32))
    elif kind == "temperature":
        in_specs += [square, div_block]
    held = pltpu.VMEM((group, lat_total + cap, LANES), jnp.float32)
    result = pl.pallas_call(
        functools.partial(legendre_kernel, kind, pair_dev, lat_groups, group),
        grid_spec=pltpu.PrefetchScalarGridSpec(
            num_scalar_prefetch=2,
            grid=(groups, group),
            in_specs=in_specs,
            out_specs=out_specs,
            scratch_shapes=[held, held],
        ),
        out_shape=out_shape,
        compiler_params=pltpu.CompilerParams(vmem_limit_bytes=VMEM_LIMIT),
        cost_estimate=pl.CostEstimate(
            flops=8 * pair_dev * row_count * lat_total * LANES,
            bytes_accessed=2 * (legendre.size + 2 * received.size),
            transcendentals=0,
        ),
        name="legendre_" + kind,
    )(counts, waves, received, legendre, lane_values, *extra)
    return result


def shards(
    grid,
    legendre,
    gauss_weights,
    band_counts,
    pair_m,
    vert_modes,
    mode_depth,
    diffusion,
    pressure_balance_matrix,
):
    lat_groups = lax.axis_size("lat")
    group = lax.axis_size("lev")
    devices = lat_groups * group
    fields, cap, levels, points = grid.shape
    pair_dev, row_count, _ = legendre.shape
    width = row_count - 1
    unit = 4 * group
    groups = -(-pair_dev // group)
    band = lax.axis_index("lat")
    owner = band * group + lax.axis_index("lev")

    table = trig_table(pair_m, width, points, devices, groups, group)

    bands = jnp.arange(lat_groups, dtype=jnp.int32)
    start = jnp.sum(jnp.where(bands < band, band_counts, 0))
    count = jnp.sum(jnp.where(bands == band, band_counts, 0))
    weights = lax.dynamic_slice(jnp.pad(gauss_weights, (0, cap)), (start,), (cap,))
    weights = jnp.where(jnp.arange(cap, dtype=jnp.int32) < count, weights / points, 0.0)
    weights = jnp.broadcast_to(weights[:, None], (cap, LANES))

    waves = lax.dynamic_slice(pair_m, (owner * pair_dev,), (pair_dev,))
    def by_lane(per_level):
        ordered = per_level.reshape((group, levels) + per_level.shape[1:])
        return jnp.swapaxes(ordered, 0, 1).reshape(per_level.shape)

    def lane_matrix(matrix):
        ordered = by_lane(by_lane(matrix).T).T
        spread = ordered[:, None, :, None] * jnp.eye(4, dtype=jnp.float32)[None, :, None, :]
        return spread.reshape(LANES, LANES)

    def lane_row(per_level):
        return jnp.repeat(by_lane(per_level), 4)[None, :]

    rows = grid.reshape(fields, cap * levels, points)
    sent = [forward(f, rows, table, weights, levels, unit) for f in range(fields)]

    def exchange(blocks):
        return lax.all_to_all(
            blocks.reshape(devices, groups, cap, LANES),
            ("lat", "lev"),
            split_axis=0,
            concat_axis=0,
            tiled=True,
        )

    received = [exchange(x) for x in sent]
    step = functools.partial(
        legendre_step, legendre=legendre, counts=band_counts, waves=waves, group=group
    )
    (vorticity,) = step(
        "vorticity", received[0], lane_values=lane_row(diffusion), extra=()
    )
    divergence, new_divergence = step(
        "divergence",
        received[1],
        lane_values=lane_row(mode_depth),
        extra=(lane_matrix(vert_modes.T), lane_matrix(vert_modes)),
    )
    (temperature,) = step(
        "temperature",
        received[2],
        lane_values=lane_row(diffusion),
        extra=(lane_matrix(pressure_balance_matrix.T), new_divergence),
    )
    out = None
    for f, made in enumerate((vorticity, divergence, temperature)):
        back = exchange(made).reshape(devices * groups, cap, LANES)
        out = inverse(f, fields, back, table, count[None], out, levels, unit)
    return out.reshape(fields, cap, levels, points)


def solution(mesh):
    placed = (
        P(None, "lat", "lev", None),
        P(("lat", "lev"), None, None),
        P(),
        P(),
        P(),
        P(),
        P(),
        P(),
        P(),
    )
    return jax.shard_map(
        shards, mesh=mesh, in_specs=placed, out_specs=P(None, "lat", "lev", None), check_vma=False
    )
```

time: 2070 us -> 743 us (0.36)
  local copies, waits for them, and re-layouts: 1190 us -> 15.7 us
  Pallas kernels: 0 us -> 276 us
  matrix products: 244 us -> 0 us
  other arithmetic: 200 us -> 15.4 us
    reshape x3 -> x5, local copies, waits for them, and re-layouts: 359 us -> 0.33 us  [the longest x3 0.17 us: by_lane(): ordered = per_level.reshape((group, levels) + per_level.shape[1:])]
    convert_element_type x2 -> x1, local copies, waits for them, and re-layouts: 343 us -> 0.14 us  [trig_table(): keep = real[:, None].astype(jnp.float32)]
    pallas_call x0 -> x10, Pallas kernels: none -> 276 us  [the longest x3 124 us: legendre_step(): pl.pallas_call(functools.partial(legendre_kernel, kind, pair_dev, lat_gro...]
    dot_general x9 -> x0, matrix products: 244 us -> none  [the longest x1 86.4 us: shards(): jnp.einsum('pkgs,glpwcfsd->pwcfldk', table_tail, arranged, preferred_elem...]
    another operation x6 -> x5, local copies, waits for them, and re-layouts: 158 us -> 2.06 us  [the longest x2 1.24 us: lane_row(): return jnp.repeat(by_lane(per_level), 4)[None, :]]
    dot_general x2 -> x0, other arithmetic: 152 us -> none  [the longest x1 76.2 us: shards(): lax.dot_general(columns, inverse_table, (((0,), (0,)), ((), ())), preferr...]
    unnamed x34 -> x10, local copies, waits for them, and re-layouts: 142 us -> 0.16 us
    slice x2 -> x0, local copies, waits for them, and re-layouts: 81 us -> none  [the longest x1 73.7 us: shards(): arranged[:, :, :, 0]]
  transfers between devices with their start and end apart: 2 -> 6, of which waited for: 2 -> 6; matrix products, arithmetic and copies ran while one was open for 11% -> 2% of each run, Pallas kernels for 0% -> 30%
where the time goes in v1:
time: 743 us; the launch traced here: 735 us
  waiting for transfers between devices  398 us (54%)
  Pallas kernels  276 us (37%)
  starting transfers between devices  27.5 us (4%)
  local copies, waits for them, and re-layouts  15.7 us (2%)
  other arithmetic  15.4 us (2%)
    all_to_all x6, waiting for transfers between devices, exchange(): lax.all_to_all(blocks.reshape(devices, groups, cap, LANES), ('lat', 'lev'...  398 us
    pallas_call x3, Pallas kernels, legendre_step(): pl.pallas_call(functools.partial(legendre_kernel, kind, pair_dev, lat_gro...  124 us
    pallas_call x3, Pallas kernels, inverse(): pl.pallas_call(functools.partial(inverse_kernel, levels, unit), grid_spec...  74.6 us
    pallas_call x3, Pallas kernels, forward(): pl.pallas_call(functools.partial(forward_kernel, levels, unit), grid=(col...  65.5 us
    all_to_all x6, starting transfers between devices, exchange(): lax.all_to_all(blocks.reshape(devices, groups, cap, LANES), ('lat', 'lev'...  27.5 us
  transfers between devices with their start and end apart: 6, of which 6 were waited for; matrix products, arithmetic and copies ran while one was open for 2% of the time, Pallas kernels for 30%

profile of v1, /device:TPU:0, one launch (start us, length us, event | category | flops | bytes accessed | tf_op | source)
XLA Modules:
  0.0 734.8 jit_solution(7979802925830775933)
XLA Ops:
  7.3 8.4 %fusion.12 = (f32[1536,128]{1,0:T(8,128)}, f32[1536,128]{1,0:T(8,128)}, f32[1536,128]{1,0:T(8,128)}, f32[1536,128]{1,0:T(8,128)}) fusion(f32[1536]{0:T(1024)S(1)} %convert_element_type.35, s32[128]{0:T(128)S(1)} %iota_multiply_fusion, s32[1536]{0:T(1024)S(1)} %mul.116, pred[1536]{0:T(1024)(128)(4,1)S(1)} %fusion.13), kind=kLoop, calls=%fused_computation.22 | loop fusion | flops 4521984 | bytes 3160064 | tf_op jit(solution)/shard_map/jit(_where)/select_n | solution.py:78
  15.7 11.9 %trig_table.1.table_ref = bf16[1536,2816]{1,0:T(8,128)(2,1)} custom-call(f32[1536,128]{1,0:T(8,128)} %get-tuple-element.12.coarse_cos, f32[1536,128]{1,0:T(8,128)} %get-tuple-element.11.coarse_sin, f32[1536,128]{1,0:T(8,128)} %get-tuple-element.14.fine_cos, f32[1536,128]{1,0:T(8,128)} %get-tuple-element.13.fine_sin), custom_call_target="tpu_custom_call" | custom-call | flops 17301504 | bytes 8650752 | tf_op jit(solution)/shard_map/trig_table/pallas_call | solution.py:66
  28.4 21.8 %forward_dft.5 = bf16[96,192,128]{2,1,0:T(8,128)(2,1)} custom-call(bf16[3,1536,2816]{2,1,0:T(8,128)(2,1)} %bitcast.74, bf16[1536,2816]{1,0:T(8,128)(2,1)} %trig_table.1.table_ref, f32[192,128]{1,0:T(8,128)} %broadcast_in_dim.57.weight_ref), custom_call_target="tpu_custom_call" | custom-call | flops 13287555072 | bytes 22020096 | tf_op jit(solution)/shard_map/forward_dft/pallas_call | solution.py:114
  50.2 7.4 %all-to-all-start.4 = ((bf16[32,3,192,128]{3,2,1,0:T(8,128)(2,1)}), bf16[32,3,192,128]{3,2,1,0:T(8,128)(2,1)}, u32[]{:S(2)}, u32[]{:S(2)}) async-start(bf16[32,3,192,128]{3,2,1,0:T(8,128)(2,1)} %bitcast.59), calls=%async_computation.4 | async-start | bytes 9437184 | tf_op jit(solution)/shard_map/all_to_all | solution.py:377
  57.6 21.8 %forward_dft.4 = bf16[96,192,128]{2,1,0:T(8,128)(2,1)} custom-call(bf16[3,1536,2816]{2,1,0:T(8,128)(2,1)} %bitcast.75, bf16[1536,2816]{1,0:T(8,128)(2,1)} %trig_table.1.table_ref, f32[192,128]{1,0:T(8,128)} %broadcast_in_dim.57.weight_ref), custom_call_target="tpu_custom_call" | custom-call | flops 13287555072 | bytes 22020096 | tf_op jit(solution)/shard_map/forward_dft/pallas_call | solution.py:114
  79.4 83.5 %all-to-all-done.4.recv_ref = bf16[32,3,192,128]{3,2,1,0:T(8,128)(2,1)} async-done(((bf16[32,3,192,128]{3,2,1,0:T(8,128)(2,1)}), bf16[32,3,192,128]{3,2,1,0:T(8,128)(2,1)}, u32[]{:S(2)}, u32[]{:S(2)}) %all-to-all-start.4) | async-done | bytes 4718624 | tf_op jit(solution)/shard_map/all_to_all | solution.py:377
  162.9 3.9 all-to-all-start.1
  166.8 21.8 %forward_dft.3 = bf16[96,192,128]{2,1,0:T(8,128)(2,1)} custom-call(bf16[3,1536,2816]{2,1,0:T(8,128)(2,1)} %bitcast.76, bf16[1536,2816]{1,0:T(8,128)(2,1)} %trig_table.1.table_ref, f32[192,128]{1,0:T(8,128)} %broadcast_in_dim.57.weight_ref), custom_call_target="tpu_custom_call" | custom-call | flops 13287555072 | bytes 22020096 | tf_op jit(solution)/shard_map/forward_dft/pallas_call | solution.py:114
  188.6 83.5 %all-to-all-done.1.recv_ref = bf16[32,3,192,128]{3,2,1,0:T(8,128)(2,1)} async-done(((bf16[32,3,192,128]{3,2,1,0:T(8,128)(2,1)}), bf16[32,3,192,128]{3,2,1,0:T(8,128)(2,1)}, u32[]{:S(2)}, u32[]{:S(2)}) %all-to-all-start.1) | async-done | bytes 4718624 | tf_op jit(solution)/shard_map/all_to_all | solution.py:377
  272.1 4.1 all-to-all-start
  278.5 32.8 %legendre_vorticity.1 = bf16[32,3,192,128]{3,2,1,0:T(8,128)(2,1)} custom-call(s32[8]{0:T(128)} %counts_ref.5, s32[12]{0:T(128)} %dynamic_slice.6.waves_ref, bf16[32,3,192,128]{3,2,1,0:T(8,128)(2,1)} %all-to-all-done.4.recv_ref, bf16[12,769,1280]{2,1,0:T(8,128)(2,1)} %leg_ref.5, f32[1,128]{1,0:T(1,128)} %broadcast_in_dim_reshape.4.rest_0_), custom_call_target="tpu_custom_call" | custom-call | flops 12095324160 | bytes 33060864 | tf_op jit(solution)/shard_map/legendre_vorticity/pallas_call | solution.py:308
  311.3 70.2 %all-to-all-done.recv_ref = bf16[32,3,192,128]{3,2,1,0:T(8,128)(2,1)} async-done(((bf16[32,3,192,128]{3,2,1,0:T(8,128)(2,1)}), bf16[32,3,192,128]{3,2,1,0:T(8,128)(2,1)}, u32[]{:S(2)}, u32[]{:S(2)}) %all-to-all-start) | async-done | bytes 4718624 | tf_op jit(solution)/shard_map/all_to_all | solution.py:377
  381.4 3.9 all-to-all-start.5
  393.7 3.8 mul.135.rest_1_
  397.5 52.4 %legendre_divergence.1 = (bf16[32,3,192,128]{3,2,1,0:T(8,128)(2,1)}, f32[12,784,128]{2,1,0:T(8,128)}) custom-call(s32[8]{0:T(128)} %counts_ref.5, s32[12]{0:T(128)} %dynamic_slice.6.waves_ref, bf16[32,3,192,128]{3,2,1,0:T(8,128)(2,1)} %all-to-all-done.1.recv_ref, bf16[12,769,1280]{2,1,0:T(8,128)(2,1)} %leg_ref.5, f32[1,128]{1,0:T(1,128)} %broadcast_in_dim_reshape.5.rest_0_, ...), custom_call_target="tpu_custom_call" | custom-call | flops 12095324160 | bytes 33060864 | tf_op jit(solution)/shard_map/legendre_divergence/pallas_call | solution.py:308
  449.9 40.7 %all-to-all-done.5 = bf16[32,3,192,128]{3,2,1,0:T(8,128)(2,1)} async-done(((bf16[32,3,192,128]{3,2,1,0:T(8,128)(2,1)}), bf16[32,3,192,128]{3,2,1,0:T(8,128)(2,1)}, u32[]{:S(2)}, u32[]{:S(2)}) %all-to-all-start.5) | async-done | bytes 4718624 | tf_op jit(solution)/shard_map/all_to_all | solution.py:377
  490.6 4.1 all-to-all-start.3
  497.0 38.7 %legendre_temperature.1 = bf16[32,3,192,128]{3,2,1,0:T(8,128)(2,1)} custom-call(s32[8]{0:T(128)} %counts_ref.5, s32[12]{0:T(128)} %dynamic_slice.6.waves_ref, bf16[32,3,192,128]{3,2,1,0:T(8,128)(2,1)} %all-to-all-done.recv_ref, bf16[12,769,1280]{2,1,0:T(8,128)(2,1)} %leg_ref.5, f32[1,128]{1,0:T(1,128)} %broadcast_in_dim_reshape.4.rest_0_, ...), custom_call_target="tpu_custom_call" | custom-call | flops 12095324160 | bytes 33060864 | tf_op jit(solution)/shard_map/legendre_temperature/pallas_call | solution.py:308
  535.7 64.3 %all-to-all-done.3 = bf16[32,3,192,128]{3,2,1,0:T(8,128)(2,1)} async-done(((bf16[32,3,192,128]{3,2,1,0:T(8,128)(2,1)}), bf16[32,3,192,128]{3,2,1,0:T(8,128)(2,1)}, u32[]{:S(2)}, u32[]{:S(2)}) %all-to-all-start.3) | async-done | bytes 4718624 | tf_op jit(solution)/shard_map/all_to_all | solution.py:377
  600.0 4.1 all-to-all-start.2
  604.2 24.9 %inverse_dft.3.rest_0_ = bf16[3,1536,2816]{2,1,0:T(8,128)(2,1)} custom-call(s32[1]{0:T(128)} %bitcast.count_ref, bf16[96,192,128]{2,1,0:T(8,128)(2,1)} %bitcast.35.spec_ref, bf16[1536,2816]{1,0:T(8,128)(2,1)} %trig_table.1.table_ref), custom_call_target="tpu_custom_call" | custom-call | flops 13287555072 | bytes 22020096 | tf_op jit(solution)/shard_map/inverse_dft/pallas_call | solution.py:170
  629.1 24.9 %inverse_dft.4.rest_0_ = bf16[3,1536,2816]{2,1,0:T(8,128)(2,1)} custom-call(s32[1]{0:T(128)} %bitcast.count_ref, bf16[96,192,128]{2,1,0:T(8,128)(2,1)} %bitcast.33.spec_ref, bf16[1536,2816]{1,0:T(8,128)(2,1)} %trig_table.1.table_ref, bf16[3,1536,2816]{2,1,0:T(8,128)(2,1)} %inverse_dft.3.rest_0_), custom_call_target="tpu_custom_call", output_to_operand_aliasing={{}: (3, {})} | custom-call | flops 13287555072 | bytes 22020096 | tf_op jit(solution)/shard_map/inverse_dft/pallas_call | solution.py:170
  653.9 55.5 %all-to-all-done.2 = bf16[32,3,192,128]{3,2,1,0:T(8,128)(2,1)} async-done(((bf16[32,3,192,128]{3,2,1,0:T(8,128)(2,1)}), bf16[32,3,192,128]{3,2,1,0:T(8,128)(2,1)}, u32[]{:S(2)}, u32[]{:S(2)}) %all-to-all-start.2) | async-done | bytes 4718624 | tf_op jit(solution)/shard_map/all_to_all | solution.py:377
  709.5 24.9 %inverse_dft.5 = bf16[3,1536,2816]{2,1,0:T(8,128)(2,1)} custom-call(s32[1]{0:T(128)} %bitcast.count_ref, bf16[96,192,128]{2,1,0:T(8,128)(2,1)} %bitcast.32.spec_ref, bf16[1536,2816]{1,0:T(8,128)(2,1)} %trig_table.1.table_ref, bf16[3,1536,2816]{2,1,0:T(8,128)(2,1)} %inverse_dft.4.rest_0_), custom_call_target="tpu_custom_call", output_to_operand_aliasing={{}: (3, {})} | custom-call | flops 13287555072 | bytes 22020096 | tf_op jit(solution)/shard_map/inverse_dft/pallas_call | solution.py:170
  (51 shorter events, 18.9 us)
Async XLA Ops:
  50.2 112.7 %all-to-all-start.4 = ((bf16[32,3,192,128]{3,2,1,0:T(8,128)(2,1)}), bf16[32,3,192,128]{3,2,1,0:T(8,128)(2,1)}, u32[]{:S(2)}, u32[]{:S(2)}) async-start(bf16[32,3,192,128]{3,2,1,0:T(8,128)(2,1)} %bitcast.59), calls=%async_computation.4 | async-start | bytes 9437184 | tf_op jit(solution)/shard_map/all_to_all | solution.py:377
  162.9 109.2 %all-to-all-start.1 = ((bf16[32,3,192,128]{3,2,1,0:T(8,128)(2,1)}), bf16[32,3,192,128]{3,2,1,0:T(8,128)(2,1)}, u32[]{:S(2)}, u32[]{:S(2)}) async-start(bf16[32,3,192,128]{3,2,1,0:T(8,128)(2,1)} %bitcast.58), calls=%async_computation.1 | async-start | bytes 9437184 | tf_op jit(solution)/shard_map/all_to_all | solution.py:377
  272.1 5.4 copy-start.2
  272.1 109.3 %all-to-all-start = ((bf16[32,3,192,128]{3,2,1,0:T(8,128)(2,1)}), bf16[32,3,192,128]{3,2,1,0:T(8,128)(2,1)}, u32[]{:S(2)}, u32[]{:S(2)}) async-start(bf16[32,3,192,128]{3,2,1,0:T(8,128)(2,1)} %bitcast.57), calls=%async_computation | async-start | bytes 9437184 | tf_op jit(solution)/shard_map/all_to_all | solution.py:377
  311.3 74.1 %copy-start.3 = (f32[32]{0:T(128)S(1)}, f32[32]{0:T(128)}, u32[]{:S(2)}) copy-start(f32[32]{0:T(128)} %param.15) | copy-start | bytes 388
  311.3 75.0 %copy-start.1 = (f32[32,32]{1,0:T(8,128)S(1)}, f32[32,32]{1,0:T(8,128)}, u32[]{:S(2)}) copy-start(f32[32,32]{1,0:T(8,128)} %param.17) | copy-start | bytes 12292
  311.3 75.3 %copy-start = (f32[32,32]{1,0:T(8,128)S(1)}, f32[32,32]{1,0:T(8,128)}, u32[]{:S(2)}) copy-start(f32[32,32]{1,0:T(8,128)} %param.14) | copy-start | bytes 12292
  381.4 109.2 %all-to-all-start.5 = ((bf16[32,3,192,128]{3,2,1,0:T(8,128)(2,1)}), bf16[32,3,192,128]{3,2,1,0:T(8,128)(2,1)}, u32[]{:S(2)}, u32[]{:S(2)}) async-start(bf16[32,3,192,128]{3,2,1,0:T(8,128)(2,1)} %legendre_vorticity.1), calls=%async_computation.5 | async-start | bytes 9437184 | tf_op jit(solution)/shard_map/all_to_all | solution.py:377
  490.6 109.4 %all-to-all-start.3 = ((bf16[32,3,192,128]{3,2,1,0:T(8,128)(2,1)}), bf16[32,3,192,128]{3,2,1,0:T(8,128)(2,1)}, u32[]{:S(2)}, u32[]{:S(2)}) async-start(bf16[32,3,192,128]{3,2,1,0:T(8,128)(2,1)} %get-tuple-element.8), calls=%async_computation.3 | async-start | bytes 9437184 | tf_op jit(solution)/shard_map/all_to_all | solution.py:377
  600.0 109.4 %all-to-all-start.2 = ((bf16[32,3,192,128]{3,2,1,0:T(8,128)(2,1)}), bf16[32,3,192,128]{3,2,1,0:T(8,128)(2,1)}, u32[]{:S(2)}, u32[]{:S(2)}) async-start(bf16[32,3,192,128]{3,2,1,0:T(8,128)(2,1)} %legendre_temperature.1), calls=%async_computation.2 | async-start | bytes 9437184 | tf_op jit(solution)/shard_map/all_to_all | solution.py:377

commit v2 on v1

v2 whole, which is shorter than its diff:
```python
import functools
import math

import jax
import jax.numpy as jnp
from jax import lax
from jax.experimental import pallas as pl
from jax.experimental.pallas import tpu as pltpu
from jax.sharding import PartitionSpec as P

LANES = 128
VMEM_LIMIT = 56 * 1024 * 1024


def swap_units(parts, unit):
    lane = lax.broadcasted_iota(jnp.int32, parts[0].shape, 1)
    step = 1
    parts = list(parts)
    while step < len(parts):
        shift = unit * step
        high = (lane & shift) != 0
        for i in range(len(parts)):
            if not i & step:
                a, b = parts[i], parts[i | step]
                parts[i] = jnp.where(high, pltpu.roll(b, shift, 1), a)
                parts[i | step] = jnp.where(high, b, pltpu.roll(a, LANES - shift, 1))
        step *= 2
    return parts


def row_tile(rows, most):
    tile = most
    while rows % tile:
        tile -= 16
    return tile


def unit_circle(wave, points):
    lane = lax.broadcasted_iota(jnp.int32, (wave.shape[0], LANES), 1).astype(jnp.float32)
    product = wave.astype(jnp.float32) * lane
    rest = product - points * jnp.floor(product * (1.0 / points))
    quarter = jnp.floor(rest * (4.0 / points) + 0.5)
    x = (rest - quarter * (points / 4.0)) * (2.0 * math.pi / points)
    y = x * x
    sine = x * (1 + y * (-1 / 6 + y * (1 / 120 + y * (-1 / 5040 + y * (1 / 362880)))))
    cosine = 1 + y * (-1 / 2 + y * (1 / 24 + y * (-1 / 720 + y * (1 / 40320))))
    odd = jnp.logical_or(quarter == 1, quarter == 3)
    cos_low = jnp.logical_or(quarter == 1, quarter == 2)
    sin_low = jnp.logical_or(quarter == 2, quarter == 3)
    cos_all = jnp.where(odd, sine, cosine)
    sin_all = jnp.where(odd, cosine, sine)
    return jnp.where(cos_low, -cos_all, cos_all), jnp.where(sin_low, -sin_all, sin_all)


def table_kernel(waves, table):
    count, points = waves.shape[0], table.shape[1]
    part = min(64, count)
    for lo in range(0, count, part):
        wave = waves[lo : lo + part, :]
        cos, sin = unit_circle(wave, points)
        cos, sin = jnp.where(wave < 0, 0.0, cos), jnp.where(wave < 0, 0.0, sin)
        half = LANES // 2
        cos_half, sin_half = cos[:, half : half + 1], sin[:, half : half + 1]
        cos_turn = jnp.broadcast_to(cos_half * cos_half - sin_half * sin_half, cos.shape)
        sin_turn = jnp.broadcast_to(2.0 * sin_half * cos_half, cos.shape)
        for a in range(points // LANES):
            both = jnp.stack(
                [cos.reshape(part // 8, 8, LANES), -sin.reshape(part // 8, 8, LANES)], axis=1
            )
            table[2 * lo : 2 * (lo + part), a * LANES : (a + 1) * LANES] = both.reshape(
                2 * part, LANES
            ).astype(table.dtype)
            cos, sin = cos * cos_turn - sin * sin_turn, sin * cos_turn + cos * sin_turn


def trig_table(pair_m, width, points, devices, groups, group):
    pair_dev = pair_m.shape[0] // devices
    lower = pair_m.reshape(devices, pair_dev)
    waves = jnp.stack([lower, width - 1 - lower], axis=2)
    waves = jnp.pad(
        waves, ((0, 0), (0, groups * group - pair_dev), (0, 0)), constant_values=-1
    )
    waves = jnp.swapaxes(waves.reshape(devices, groups, 2 * group), 0, 1).reshape(-1, 1)
    count = waves.shape[0]
    tile = LANES if count % LANES == 0 else count
    return pl.pallas_call(
        table_kernel,
        grid=(count // tile,),
        in_specs=[pl.BlockSpec((tile, 1), lambda t: (t, 0))],
        out_specs=pl.BlockSpec((2 * tile, points), lambda t: (t, 0)),
        out_shape=jax.ShapeDtypeStruct((2 * count, points), jnp.bfloat16),
        cost_estimate=pl.CostEstimate(
            flops=8 * count * points, bytes_accessed=4 * count * points, transcendentals=0
        ),
        name="trig_table",
    )(waves)


def forward_kernel(levels, unit, grid_ref, table_ref, weight_ref, out_ref, scratch):
    cols = table_ref.shape[0]
    rows = grid_ref.shape[1]
    cap = rows // levels
    tall = cap // 2 if cap % 32 == 0 else cap
    tile = row_tile(tall, 32)
    for r in range(0, cap, tall):
        values = lax.dot_general(
            grid_ref[0, r * levels : (r + tall) * levels, :],
            table_ref[...],
            (((1,), (1,)), ((), ())),
            preferred_element_type=jnp.float32,
        )
        for n in range(cols // LANES):
            scratch[n, r * levels : (r + tall) * levels, :] = values[
                :, n * LANES : (n + 1) * LANES
            ]
        for s in range(r, r + tall, tile):
            weight = weight_ref[s : s + tile, :]
            for n in range(cols // LANES):
                parts = [
                    scratch[n, pl.ds(s * levels + l, tile, stride=levels), :] * weight
                    for l in range(levels)
                ]
                for a, part in enumerate(swap_units(parts, unit)):
                    out_ref[n * levels + a, 0, s : s + tile, :] = part.astype(jnp.bfloat16)


def forward(field, first, count, grid, table, weights, levels, unit, devices):
    _, rows, points = grid.shape
    cap = rows // levels
    wide = 2 * levels if devices % (2 * levels) == 0 else levels
    steps = devices // wide
    columns = count * devices * unit
    return pl.pallas_call(
        functools.partial(forward_kernel, levels, unit),
        grid=(count, steps),
        in_specs=[
            pl.BlockSpec((1, rows, points), lambda i, t: (field, 0, 0)),
            pl.BlockSpec((wide * unit, points), lambda i, t: ((first + i) * steps + t, 0)),
            pl.BlockSpec((cap, LANES), lambda i, t: (0, 0)),
        ],
        out_specs=pl.BlockSpec((wide, 1, cap, LANES), lambda i, t: (t, i, 0, 0)),
        out_shape=jax.ShapeDtypeStruct((devices, count, cap, LANES), jnp.bfloat16),
        scratch_shapes=[pltpu.VMEM((wide * unit // LANES, rows, LANES), jnp.float32)],
        compiler_params=pltpu.CompilerParams(vmem_limit_bytes=VMEM_LIMIT),
        cost_estimate=pl.CostEstimate(
            flops=2 * rows * points * columns,
            bytes_accessed=2 * (rows * points + columns * points + rows * columns),
            transcendentals=0,
        ),
        name="forward_dft",
    )(grid, table, weights)


def inverse_kernel(levels, unit, first_row, count_ref, spec_ref, table_ref, *rest):
    out_ref, turned, columns = rest[-3:]
    devices, groups, cap, _ = spec_ref.shape
    tile = row_tile(cap, 32)
    rows = tile * levels
    blocks = [(i, d) for i in range(groups) for d in range(0, devices, levels)]

    @pl.when(pl.program_id(0) == 0)
    def _():
        @pl.loop(0, cap // tile)
        def _(r):
            at = pl.ds(pl.multiple_of(r * tile, tile), tile)
            for n, (i, d) in enumerate(blocks):
                parts = [spec_ref[d + a, i, at, :].astype(jnp.float32) for a in range(levels)]
                for l, part in enumerate(swap_units(parts, unit)):
                    turned[n, pl.ds(l, tile, stride=levels), :] = part
            row = r * rows + lax.broadcasted_iota(jnp.int32, (rows, LANES), 0)
            valid = row < (count_ref[0] - first_row) * levels
            lines = pl.ds(pl.multiple_of(r * rows, rows), rows)
            for n in range(len(blocks)):
                columns[lines, n * LANES : (n + 1) * LANES] = jnp.where(
                    valid, turned[n], 0.0
                ).astype(jnp.bfloat16)

    out_ref[0] = jnp.dot(
        columns[...], table_ref[...], preferred_element_type=jnp.float32
    ).astype(out_ref.dtype)


def inverse(field, first_row, spec, table, count, partial, shape, levels, unit):
    devices, groups, cap, _ = spec.shape
    columns, points = table.shape
    rows = cap * levels
    tile = row_tile(cap, 32)
    wide = 2 * LANES if points % (2 * LANES) == 0 else LANES
    in_specs = [
        pl.BlockSpec((devices, groups, cap, LANES), lambda t, c: (0, 0, 0, 0)),
        pl.BlockSpec((columns, wide), lambda t, c: (0, t)),
    ]
    operands = [spec, table]
    if partial is not None:
        in_specs.append(pl.BlockSpec(memory_space=pl.ANY))
        operands.append(partial)
    return pl.pallas_call(
        functools.partial(inverse_kernel, levels, unit, first_row),
        grid_spec=pltpu.PrefetchScalarGridSpec(
            num_scalar_prefetch=1,
            grid=(points // wide,),
            in_specs=in_specs,
            out_specs=pl.BlockSpec((1, rows, wide), lambda t, c: (field, first_row // cap, t)),
            scratch_shapes=[
                pltpu.VMEM((columns // LANES, tile * levels, LANES), jnp.float32),
                pltpu.VMEM((rows, columns), jnp.bfloat16),
            ],
        ),
        out_shape=jax.ShapeDtypeStruct(shape, jnp.bfloat16),
        input_output_aliases={} if partial is None else {3: 0},
        compiler_params=pltpu.CompilerParams(vmem_limit_bytes=VMEM_LIMIT),
        cost_estimate=pl.CostEstimate(
            flops=2 * rows * points * columns,
            bytes_accessed=2 * (rows * points + columns * points + rows * columns),
            transcendentals=0,
        ),
        name="inverse_dft",
    )(count, *operands)


def legendre_kernel(
    kind, first, pair_dev, lat_groups, group, outs, counts_ref, waves_ref, recv_ref, leg_ref, *rest
):
    lane_ref = rest[0]
    gathered, made = rest[-2:]
    if kind == "divergence":
        to_modes, from_modes = rest[1:3]
        div_out = rest[-3]
        out_refs = rest[-3 - outs : -3]
    else:
        out_refs = rest[-2 - outs : -2]
    if kind == "temperature":
        balance, div_in = rest[1:3]
    row_count, lat_total = leg_ref.shape[1:]
    width = row_count - 1
    cap = recv_ref.shape[2]
    member = pl.program_id(1)
    pair = (first + pl.program_id(0)) * group + member

    @pl.when(member == 0)
    def _():
        start = 0
        for g in range(lat_groups):
            parts = [recv_ref[g * group + h, 0].astype(jnp.float32) for h in range(group)]
            for b, part in enumerate(swap_units(parts, 2)):
                gathered[b, pl.ds(start, cap), :] = part
            start = start + counts_ref[g]

    @pl.when(pair < pair_dev)
    def _():
        wave = waves_ref[pair]
        coeffs = gathered[member, :lat_total, :].astype(jnp.bfloat16)
        main = leg_ref[0, :width, :]
        last = jnp.broadcast_to(leg_ref[0, width:, :], (16, lat_total))
        spectral = jnp.concatenate(
            [
                jnp.dot(main, coeffs, preferred_element_type=jnp.float32),
                jnp.dot(last, coeffs, preferred_element_type=jnp.float32),
            ],
            axis=0,
        )
        shape = spectral.shape
        row = lax.broadcasted_iota(jnp.int32, shape, 0)
        lane = lax.broadcasted_iota(jnp.int32, shape, 1)
        own = row < width - wave
        upper = (lane & 1) != 0
        keep = jnp.logical_and(jnp.logical_xor(own, upper), row < row_count)
        degree = jnp.where(own, row + wave, row - 1)
        ratio = (degree * (degree + 1)).astype(jnp.float32) / float(width * (width - 1))
        spectral = jnp.where(keep, spectral, 0.0)
        exact = functools.partial(
            jnp.dot, precision=lax.Precision.HIGHEST, preferred_element_type=jnp.float32
        )
        if kind == "vorticity":
            new = spectral / (1.0 + lane_ref[...] * ratio * ratio)
        elif kind == "divergence":
            modes = exact(spectral, to_modes[...])
            modes = modes / (1.0 + lane_ref[...] * ratio)
            new = exact(modes, from_modes[...])
            div_out[0] = new
        else:
            new = spectral - exact(div_in[0], balance[...])
        zonal = jnp.logical_and(wave == 0, jnp.logical_not(upper))
        new = new * jnp.where(zonal, 1.0, 2.0)
        tail = jnp.concatenate(
            [new[width:], jnp.zeros((LANES - 16, LANES), jnp.float32)], axis=0
        )
        turned = jnp.dot(
            new[:width].T.astype(jnp.bfloat16), main, preferred_element_type=jnp.float32
        )
        turned += jnp.dot(
            tail.T.astype(jnp.bfloat16),
            jnp.broadcast_to(leg_ref[0, width:, :], (LANES, lat_total)),
            preferred_element_type=jnp.float32,
        )
        made[member, :lat_total, :] = turned.T
        made[member, lat_total:, :] = jnp.zeros((cap, LANES), jnp.float32)

    @pl.when(pair >= pair_dev)
    def _():
        made[member] = jnp.zeros(made.shape[1:], jnp.float32)

    @pl.when(member == group - 1)
    def _():
        start = 0
        for g in range(lat_groups):
            parts = [made[b, pl.ds(start, cap), :] for b in range(group)]
            for h, part in enumerate(swap_units(parts, 2)):
                row = 0
                for out_ref in out_refs:
                    size = out_ref.shape[2]
                    out_ref[g * group + h, 0] = part[row : row + size].astype(jnp.bfloat16)
                    row += size
            start = start + counts_ref[g]


def legendre_step(
    kind, first, groups, splits, received, legendre, counts, waves, lane_values, extra, group, partial
):
    devices, some, cap, _ = received.shape
    pair_dev, row_count, lat_total = legendre.shape
    lat_groups = devices // group

    def at_pair(i, b, *_):
        return (jnp.minimum((first + i) * group + b, pair_dev - 1), 0, 0)

    def whole(i, b, *_):
        return (0, 0)

    square = pl.BlockSpec((LANES, LANES), whole)
    div_block = pl.BlockSpec((1, row_count + 15, LANES), at_pair)
    in_specs = [
        pl.BlockSpec((devices, 1, cap, LANES), lambda i, b, *_: (0, i, 0, 0)),
        pl.BlockSpec((1, row_count, lat_total), at_pair),
        pl.BlockSpec((1, LANES), whole),
    ]
    out_specs = [
        pl.BlockSpec((devices, 1, size, LANES), lambda i, b, *_: (0, first + i, 0, 0))
        for size in splits
    ]
    out_shape = [
        jax.ShapeDtypeStruct((devices, groups, size, LANES), jnp.bfloat16) for size in splits
    ]
    if kind == "divergence":
        in_specs += [square, square]
        out_specs.append(div_block)
        out_shape.append(jax.ShapeDtypeStruct((pair_dev, row_count + 15, LANES), jnp.float32))
    elif kind == "temperature":
        in_specs += [square, div_block]
    operands = [counts, waves, received, legendre, lane_values, *extra]
    aliases = {}
    if partial is not None:
        aliases = {len(operands): 0}
        in_specs.append(pl.BlockSpec(memory_space=pl.ANY))
        operands.append(partial)
    held = pltpu.VMEM((group, lat_total + cap, LANES), jnp.float32)
    return pl.pallas_call(
        functools.partial(legendre_kernel, kind, first, pair_dev, lat_groups, group, len(splits)),
        grid_spec=pltpu.PrefetchScalarGridSpec(
            num_scalar_prefetch=2,
            grid=(some, group),
            in_specs=in_specs,
            out_specs=out_specs,
            scratch_shapes=[held, held],
        ),
        out_shape=out_shape,
        input_output_aliases=aliases,
        compiler_params=pltpu.CompilerParams(vmem_limit_bytes=VMEM_LIMIT),
        cost_estimate=pl.CostEstimate(
            flops=8 * some * group * row_count * lat_total * LANES,
            bytes_accessed=2 * (some * group * row_count * lat_total + 2 * received.size),
            transcendentals=0,
        ),
        name="legendre_" + kind,
    )(*operands)


def shards(
    grid,
    legendre,
    gauss_weights,
    band_counts,
    pair_m,
    vert_modes,
    mode_depth,
    diffusion,
    pressure_balance_matrix,
):
    lat_groups = lax.axis_size("lat")
    group = lax.axis_size("lev")
    devices = lat_groups * group
    fields, cap, levels, points = grid.shape
    pair_dev, row_count, _ = legendre.shape
    width = row_count - 1
    unit = 4 * group
    groups = -(-pair_dev // group)
    band = lax.axis_index("lat")
    owner = band * group + lax.axis_index("lev")

    table = trig_table(pair_m, width, points, devices, groups, group)

    bands = jnp.arange(lat_groups, dtype=jnp.int32)
    start = jnp.sum(jnp.where(bands < band, band_counts, 0))
    count = jnp.sum(jnp.where(bands == band, band_counts, 0))
    weights = lax.dynamic_slice(jnp.pad(gauss_weights, (0, cap)), (start,), (cap,))
    weights = jnp.where(jnp.arange(cap, dtype=jnp.int32) < count, weights / points, 0.0)
    weights = jnp.broadcast_to(weights[:, None], (cap, LANES))

    waves = lax.dynamic_slice(pair_m, (owner * pair_dev,), (pair_dev,))

    def lane_row(per_level):
        ordered = per_level.reshape(group, levels).T[:, None, :, None]
        return jnp.broadcast_to(ordered, (levels, 2, group, 2)).reshape(1, LANES)

    def lane_matrix(matrix):
        ordered = matrix.reshape(group, levels, group, levels).transpose(1, 0, 3, 2)
        two = jnp.eye(2, dtype=jnp.float32)
        spread = jnp.einsum("ahbk,pq,vw->aphvbqkw", ordered, two, two, precision="highest")
        return spread.reshape(LANES, LANES)

    rows = grid.reshape(fields, cap * levels, points)

    def exchange(blocks):
        return lax.all_to_all(
            blocks, ("lat", "lev"), split_axis=0, concat_axis=0, tiled=True
        )

    plan = [(0, 0, 1), (0, 1, groups - 1)] if groups > 1 else [(0, 0, groups)]
    plan += [(f, 0, groups) for f in range(1, fields)]
    received = []
    for field, first, some in plan:
        sent = forward(field, first, some, rows, table, weights, levels, unit, devices)
        weights, _ = lax.optimization_barrier((weights, sent))
        received.append((first, exchange(sent)))

    step = functools.partial(
        legendre_step, groups=groups, legendre=legendre, counts=band_counts, waves=waves, group=group
    )
    late = max(16, cap // 3 // 16 * 16) if cap > 16 else 0
    pieces = (cap - late, late) if late and (cap - late) % late == 0 else (cap,)
    vorticity = None
    for first, blocks in received[:-2]:
        (vorticity,) = step(
            "vorticity",
            first,
            splits=(cap,),
            received=blocks,
            lane_values=lane_row(diffusion),
            extra=(),
            partial=vorticity,
        )
    divergence, new_divergence = step(
        "divergence",
        0,
        splits=(cap,),
        received=received[-2][1],
        lane_values=lane_row(mode_depth),
        extra=(lane_matrix(vert_modes.T), lane_matrix(vert_modes)),
        partial=None,
    )
    temperature = step(
        "temperature",
        0,
        splits=pieces,
        received=received[-1][1],
        lane_values=lane_row(diffusion),
        extra=(lane_matrix(pressure_balance_matrix.T), new_divergence),
        partial=None,
    )
    out = None
    back = [(0, 0, vorticity), (1, 0, divergence)]
    for n, made in enumerate(temperature):
        back.append((2, sum(pieces[:n]), made))
    for field, first_row, made in back:
        out = inverse(
            field,
            first_row,
            exchange(made),
            table,
            count[None],
            out,
            (fields, cap * levels, points),
            levels,
            unit,
        )
    return out.reshape(fields, cap, levels, points)


def solution(mesh):
    placed = (
        P(None, "lat", "lev", None),
        P(("lat", "lev"), None, None),
        P(),
        P(),
        P(),
        P(),
        P(),
        P(),
        P(),
    )
    return jax.shard_map(
        shards, mesh=mesh, in_specs=placed, out_specs=P(None, "lat", "lev", None), check_vma=False
    )
```

time: 743 us -> 793 us (1.067)
  blocking collectives: 0 us -> 186 us
  waiting for transfers between devices: 398 us -> 217 us
  Pallas kernels: 276 us -> 315 us
  local copies, waits for them, and re-layouts: 15.7 us -> 29.4 us
    all_to_all x0 -> x2, blocking collectives: none -> 186 us  [exchange(): lax.all_to_all(blocks, ('lat', 'lev'), split_axis=0, concat_axis=0, tiled...]
    all_to_all x6, waiting for transfers between devices: 398 us -> 217 us  [exchange(): lax.all_to_all(blocks, ('lat', 'lev'), split_axis=0, concat_axis=0, tiled...]
    pallas_call x10 -> x13, Pallas kernels: 276 us -> 315 us  [the longest x4 128 us: legendre_step(): pl.pallas_call(functools.partial(legendre_kernel, kind, first, pair_dev,...]
    reshape x5 -> x11, local copies, waits for them, and re-layouts: 0.33 us -> 21.2 us  [the longest x3 18.5 us: lane_matrix(): return spread.reshape(LANES, LANES)]
    mul x4 -> x0, local copies, waits for them, and re-layouts: 10.1 us -> none  [the longest x3 9.96 us: lane_matrix(): ordered[:, None, :, None] * jnp.eye(4, dtype=jnp.float32)[None, :, None, :]]
    select_n x1 -> x0, other arithmetic: 8.37 us -> none  [trig_table(): jnp.where(sine, cos_a, sin_a)]
  transfers between devices with their start and end apart: 6 -> 6, of which waited for: 6 -> 4; matrix products, arithmetic and copies ran while one was open for 2% -> 4% of each run, Pallas kernels for 30% -> 36%
where the time goes in v2:
time: 793 us; the launch traced here: 784 us
  Pallas kernels  315 us (40%)
  waiting for transfers between devices  217 us (27%)
  blocking collectives  186 us (23%)
  local copies, waits for them, and re-layouts  29.4 us (4%)
  starting transfers between devices  26.5 us (3%)
    all_to_all x6, waiting for transfers between devices, exchange(): lax.all_to_all(blocks, ('lat', 'lev'), split_axis=0, concat_axis=0, tiled...  217 us
    all_to_all x2, blocking collectives, exchange(): lax.all_to_all(blocks, ('lat', 'lev'), split_axis=0, concat_axis=0, tiled...  186 us
    pallas_call x4, Pallas kernels, legendre_step(): pl.pallas_call(functools.partial(legendre_kernel, kind, first, pair_dev,...  128 us
    pallas_call x4, Pallas kernels, inverse(): pl.pallas_call(functools.partial(inverse_kernel, levels, unit, first_row)...  105 us
    pallas_call x4, Pallas kernels, forward(): pl.pallas_call(functools.partial(forward_kernel, levels, unit), grid=(cou...  74.9 us
    all_to_all x6, starting transfers between devices, exchange(): lax.all_to_all(blocks, ('lat', 'lev'), split_axis=0, concat_axis=0, tiled...  26.5 us
    reshape x3, local copies, waits for them, and re-layouts, lane_matrix(): return spread.reshape(LANES, LANES)  18.5 us
  transfers between devices with their start and end apart: 6, of which 4 were waited for; matrix products, arithmetic and copies ran while one was open for 4% of the time, Pallas kernels for 36%

profile of v2, /device:TPU:0, one launch (start us, length us, event | category | flops | bytes accessed | tf_op | source)
XLA Modules:
  0.0 784.3 jit_solution(18326251199443359148)
XLA Ops:
  4.6 7.2 trig_table.1.table_ref
  13.7 10.9 %forward_dft.4 = bf16[32,1,192,128]{3,2,1,0:T(8,128)(2,1)} custom-call(bf16[3,1536,2816]{2,1,0:T(8,128)(2,1)} %bitcast.23, bf16[1536,2816]{1,0:T(8,128)(2,1)} %trig_table.1.table_ref, f32[192,128]{1,0:T(8,128)} %broadcast_in_dim.20.weight_ref), custom_call_target="tpu_custom_call" | custom-call | flops 4429185024 | bytes 13107200 | tf_op jit(solution)/shard_map/forward_dft/pallas_call | solution.py:133
  24.7 7.3 all-to-all-start.6
  32.0 17.2 %forward_dft.5 = bf16[32,2,192,128]{3,2,1,0:T(8,128)(2,1)} custom-call(bf16[3,1536,2816]{2,1,0:T(8,128)(2,1)} %bitcast.24, bf16[1536,2816]{1,0:T(8,128)(2,1)} %trig_table.1.table_ref, f32[192,128]{1,0:T(8,128)} %broadcast_in_dim.20.weight_ref), custom_call_target="tpu_custom_call" | custom-call | flops 8858370048 | bytes 17563648 | tf_op jit(solution)/shard_map/forward_dft/pallas_call | solution.py:133
  49.2 20.5 %all-to-all-done.6.recv_ref = bf16[32,1,192,128]{3,2,1,0:T(8,128)(2,1)S(1)} async-done(((bf16[32,1,192,128]{3,2,1,0:T(8,128)(2,1)}), bf16[32,1,192,128]{3,2,1,0:T(8,128)(2,1)S(1)}, u32[]{:S(2)}, u32[]{:S(2)}) %all-to-all-start.6) | async-done | bytes 1572896 | tf_op jit(solution)/shard_map/all_to_all | solution.py:424
  74.7 23.4 %forward_dft.6 = bf16[32,3,192,128]{3,2,1,0:T(8,128)(2,1)} custom-call(bf16[3,1536,2816]{2,1,0:T(8,128)(2,1)} %bitcast.25, bf16[1536,2816]{1,0:T(8,128)(2,1)} %trig_table.1.table_ref, f32[192,128]{1,0:T(8,128)} %broadcast_in_dim.20.weight_ref), custom_call_target="tpu_custom_call" | custom-call | flops 13287555072 | bytes 22020096 | tf_op jit(solution)/shard_map/forward_dft/pallas_call | solution.py:133
  98.1 48.1 %all-to-all-done.5.recv_ref = bf16[32,2,192,128]{3,2,1,0:T(8,128)(2,1)S(1)} async-done(((bf16[32,2,192,128]{3,2,1,0:T(8,128)(2,1)}), bf16[32,2,192,128]{3,2,1,0:T(8,128)(2,1)S(1)}, u32[]{:S(2)}, u32[]{:S(2)}) %all-to-all-start.5) | async-done | bytes 3145760 | tf_op jit(solution)/shard_map/all_to_all | solution.py:424
  151.9 23.3 %forward_dft.7 = bf16[32,3,192,128]{3,2,1,0:T(8,128)(2,1)} custom-call(bf16[3,1536,2816]{2,1,0:T(8,128)(2,1)} %bitcast.26, bf16[1536,2816]{1,0:T(8,128)(2,1)} %trig_table.1.table_ref, f32[192,128]{1,0:T(8,128)} %broadcast_in_dim.20.weight_ref), custom_call_target="tpu_custom_call" | custom-call | flops 13287555072 | bytes 22020096 | tf_op jit(solution)/shard_map/forward_dft/pallas_call | solution.py:133
  175.3 82.0 %all-to-all-done.1.recv_ref = bf16[32,3,192,128]{3,2,1,0:T(8,128)(2,1)} async-done(((bf16[32,3,192,128]{3,2,1,0:T(8,128)(2,1)}), bf16[32,3,192,128]{3,2,1,0:T(8,128)(2,1)}, u32[]{:S(2)}, u32[]{:S(2)}) %all-to-all-start.1) | async-done | bytes 4718624 | tf_op jit(solution)/shard_map/all_to_all | solution.py:424
  263.5 13.4 %legendre_vorticity.2.rest_1_ = bf16[32,3,192,128]{3,2,1,0:T(8,128)(2,1)} custom-call(s32[8]{0:T(128)} %counts_ref.7, s32[12]{0:T(128)} %dynamic_slice.6.waves_ref, bf16[32,1,192,128]{3,2,1,0:T(8,128)(2,1)} %copy-done.1, bf16[12,769,1280]{2,1,0:T(8,128)(2,1)} %leg_ref.7, f32[1,128]{1,0:T(1,128)} %reshape.64.rest_0_), custom_call_target="tpu_custom_call" | custom-call | flops 4031774720 | bytes 11020288 | tf_op jit(solution)/shard_map/legendre_vorticity/pallas_call | solution.py:357
  276.9 23.3 %legendre_vorticity.3 = bf16[32,3,192,128]{3,2,1,0:T(8,128)(2,1)} custom-call(s32[8]{0:T(128)} %counts_ref.7, s32[12]{0:T(128)} %dynamic_slice.6.waves_ref, bf16[32,2,192,128]{3,2,1,0:T(8,128)(2,1)} %copy-done, bf16[12,769,1280]{2,1,0:T(8,128)(2,1)} %leg_ref.7, f32[1,128]{1,0:T(1,128)} %reshape.64.rest_0_, ...), custom_call_target="tpu_custom_call", output_to_operand_aliasing={{}: (5, {})} | custom-call | flops 8063549440 | bytes 22040576 | tf_op jit(solution)/shard_map/legendre_vorticity/pallas_call | solution.py:357
  300.2 66.4 %all-to-all-done.recv_ref = bf16[32,3,192,128]{3,2,1,0:T(8,128)(2,1)} async-done(((bf16[32,3,192,128]{3,2,1,0:T(8,128)(2,1)}), bf16[32,3,192,128]{3,2,1,0:T(8,128)(2,1)}, u32[]{:S(2)}, u32[]{:S(2)}) %all-to-all-start) | async-done | bytes 4718624 | tf_op jit(solution)/shard_map/all_to_all | solution.py:424
  372.7 5.6 multiply_bitcast_fusion
  378.3 6.2 reshape.72.rest_2_
  384.5 6.2 reshape.70.rest_1_
  390.7 6.2 reshape.66.rest_1_
  396.9 52.4 %legendre_divergence.1 = (bf16[32,3,192,128]{3,2,1,0:T(8,128)(2,1)}, f32[12,784,128]{2,1,0:T(8,128)}) custom-call(s32[8]{0:T(128)} %counts_ref.7, s32[12]{0:T(128)} %dynamic_slice.6.waves_ref, bf16[32,3,192,128]{3,2,1,0:T(8,128)(2,1)} %all-to-all-done.1.recv_ref, bf16[12,769,1280]{2,1,0:T(8,128)(2,1)} %leg_ref.7, f32[1,128]{1,0:T(1,128)} %reshape.68.rest_0_, ...), custom_call_target="tpu_custom_call" | custom-call | flops 12095324160 | bytes 33060864 | tf_op jit(solution)/shard_map/legendre_divergence/pallas_call | solution.py:357
  449.3 38.9 %legendre_temperature.1 = (bf16[32,3,128,128]{3,2,1,0:T(8,128)(2,1)}, bf16[32,3,64,128]{3,2,1,0:T(8,128)(2,1)}) custom-call(s32[8]{0:T(128)} %counts_ref.7, s32[12]{0:T(128)} %dynamic_slice.6.waves_ref, bf16[32,3,192,128]{3,2,1,0:T(8,128)(2,1)} %all-to-all-done.recv_ref, bf16[12,769,1280]{2,1,0:T(8,128)(2,1)} %leg_ref.7, f32[1,128]{1,0:T(1,128)} %reshape.64.rest_0_, ...), custom_call_target="tpu_custom_call" | custom-call | flops 12095324160 | bytes 33060864 | tf_op jit(solution)/shard_map/legendre_temperature/pallas_call | solution.py:357
  488.2 77.3 %all_to_all.40.spec_ref = bf16[32,3,128,128]{3,2,1,0:T(8,128)(2,1)} all-to-all(bf16[32,3,128,128]{3,2,1,0:T(8,128)(2,1)} %get-tuple-element.17), channel_id=1, replica_groups=mesh['lat'=8,'lev'=4] {'lat','lev'}, dimensions={0} | all-to-all | bytes 6291456 | tf_op jit(solution)/shard_map/all_to_all | solution.py:424
  565.5 109.0 %all_to_all.41.spec_ref = bf16[32,3,192,128]{3,2,1,0:T(8,128)(2,1)} all-to-all(bf16[32,3,192,128]{3,2,1,0:T(8,128)(2,1)S(1)} %copy-done.3), channel_id=1, replica_groups=mesh['lat'=8,'lev'=4] {'lat','lev'}, dimensions={0} | all-to-all | bytes 9437184 | tf_op jit(solution)/shard_map/all_to_all | solution.py:424
  677.7 31.9 %inverse_dft.4.rest_0_ = bf16[3,1536,2816]{2,1,0:T(8,128)(2,1)} custom-call(s32[1]{0:T(128)} %bitcast.count_ref, bf16[32,3,192,128]{3,2,1,0:T(8,128)(2,1)} %all-to-all-done.7.spec_ref, bf16[1536,2816]{1,0:T(8,128)(2,1)} %trig_table.1.table_ref), custom_call_target="tpu_custom_call" | custom-call | flops 13287555072 | bytes 22020096 | tf_op jit(solution)/shard_map/inverse_dft/pallas_call | solution.py:197
  709.6 31.9 %inverse_dft.5.rest_0_ = bf16[3,1536,2816]{2,1,0:T(8,128)(2,1)} custom-call(s32[1]{0:T(128)} %bitcast.count_ref, bf16[32,3,192,128]{3,2,1,0:T(8,128)(2,1)} %all_to_all.41.spec_ref, bf16[1536,2816]{1,0:T(8,128)(2,1)} %trig_table.1.table_ref, bf16[3,1536,2816]{2,1,0:T(8,128)(2,1)} %inverse_dft.4.rest_0_), custom_call_target="tpu_custom_call", output_to_operand_aliasing={{}: (3, {})} | custom-call | flops 13287555072 | bytes 22020096 | tf_op jit(solution)/shard_map/inverse_dft/pallas_call | solution.py:197
  741.5 24.4 %inverse_dft.6.rest_0_ = bf16[3,1536,2816]{2,1,0:T(8,128)(2,1)} custom-call(s32[1]{0:T(128)} %bitcast.count_ref, bf16[32,3,128,128]{3,2,1,0:T(8,128)(2,1)} %all_to_all.40.spec_ref, bf16[1536,2816]{1,0:T(8,128)(2,1)} %trig_table.1.table_ref, bf16[3,1536,2816]{2,1,0:T(8,128)(2,1)} %inverse_dft.5.rest_0_), custom_call_target="tpu_custom_call", output_to_operand_aliasing={{}: (3, {})} | custom-call | flops 8858370048 | bytes 17563648 | tf_op jit(solution)/shard_map/inverse_dft/pallas_call | solution.py:197
  767.1 16.8 %inverse_dft.7 = bf16[3,1536,2816]{2,1,0:T(8,128)(2,1)} custom-call(s32[1]{0:T(128)} %bitcast.count_ref, bf16[32,3,64,128]{3,2,1,0:T(8,128)(2,1)} %copy-done.2, bf16[1536,2816]{1,0:T(8,128)(2,1)} %trig_table.1.table_ref, bf16[3,1536,2816]{2,1,0:T(8,128)(2,1)} %inverse_dft.6.rest_0_), custom_call_target="tpu_custom_call", output_to_operand_aliasing={{}: (3, {})} | custom-call | flops 4429185024 | bytes 13107200 | tf_op jit(solution)/shard_map/inverse_dft/pallas_call | solution.py:197
  (52 shorter events, 32.1 us)
Async XLA Ops:
  4.6 7.8 copy-start.6
  24.7 45.1 %all-to-all-start.6 = ((bf16[32,1,192,128]{3,2,1,0:T(8,128)(2,1)}), bf16[32,1,192,128]{3,2,1,0:T(8,128)(2,1)S(1)}, u32[]{:S(2)}, u32[]{:S(2)}) async-start(bf16[32,1,192,128]{3,2,1,0:T(8,128)(2,1)} %forward_dft.4), calls=%async_computation.6 | async-start | bytes 3145728 | tf_op jit(solution)/shard_map/all_to_all | solution.py:424
  69.7 1.2 copy-start.1
  70.9 75.2 %all-to-all-start.5 = ((bf16[32,2,192,128]{3,2,1,0:T(8,128)(2,1)}), bf16[32,2,192,128]{3,2,1,0:T(8,128)(2,1)S(1)}, u32[]{:S(2)}, u32[]{:S(2)}) async-start(bf16[32,2,192,128]{3,2,1,0:T(8,128)(2,1)} %forward_dft.5), calls=%async_computation.5 | async-start | bytes 6291456 | tf_op jit(solution)/shard_map/all_to_all | solution.py:424
  146.1 1.7 copy-start
  147.8 109.4 %all-to-all-start.1 = ((bf16[32,3,192,128]{3,2,1,0:T(8,128)(2,1)}), bf16[32,3,192,128]{3,2,1,0:T(8,128)(2,1)}, u32[]{:S(2)}, u32[]{:S(2)}) async-start(bf16[32,3,192,128]{3,2,1,0:T(8,128)(2,1)} %forward_dft.6), calls=%async_computation.1 | async-start | bytes 9437184 | tf_op jit(solution)/shard_map/all_to_all | solution.py:424
  175.2 87.3 %copy-start.7 = (f32[32]{0:T(128)S(1)}, f32[32]{0:T(128)}, u32[]{:S(2)}) copy-start(f32[32]{0:T(128)} %param.16) | copy-start | bytes 388
  257.2 109.3 %all-to-all-start = ((bf16[32,3,192,128]{3,2,1,0:T(8,128)(2,1)}), bf16[32,3,192,128]{3,2,1,0:T(8,128)(2,1)}, u32[]{:S(2)}, u32[]{:S(2)}) async-start(bf16[32,3,192,128]{3,2,1,0:T(8,128)(2,1)} %forward_dft.7), calls=%async_computation | async-start | bytes 9437184 | tf_op jit(solution)/shard_map/all_to_all | solution.py:424
  300.2 70.5 %copy-start.8 = (f32[32]{0:T(128)S(1)}, f32[32]{0:T(128)}, u32[]{:S(2)}) copy-start(f32[32]{0:T(128)} %param.15) | copy-start | bytes 388
  300.2 71.4 %copy-start.5 = (f32[32,32]{1,0:T(8,128)S(1)}, f32[32,32]{1,0:T(8,128)}, u32[]{:S(2)}) copy-start(f32[32,32]{1,0:T(8,128)} %param.17) | copy-start | bytes 12292
  300.2 71.8 %copy-start.4 = (f32[32,32]{1,0:T(8,128)S(1)}, f32[32,32]{1,0:T(8,128)}, u32[]{:S(2)}) copy-start(f32[32,32]{1,0:T(8,128)} %param.14) | copy-start | bytes 12292
  366.5 121.7 %all-to-all-start.7 = ((bf16[32,3,192,128]{3,2,1,0:T(8,128)(2,1)}), bf16[32,3,192,128]{3,2,1,0:T(8,128)(2,1)}, u32[]{:S(2)}, u32[]{:S(2)}) async-start(bf16[32,3,192,128]{3,2,1,0:T(8,128)(2,1)} %legendre_vorticity.3), calls=%async_computation.7 | async-start | bytes 9437184 | tf_op jit(solution)/shard_map/all_to_all | solution.py:424
  488.2 77.3 %copy-start.3 = (bf16[32,3,192,128]{3,2,1,0:T(8,128)(2,1)S(1)}, bf16[32,3,192,128]{3,2,1,0:T(8,128)(2,1)}, u32[]{:S(2)}) copy-start(bf16[32,3,192,128]{3,2,1,0:T(8,128)(2,1)} %get-tuple-element.18) | copy-start | bytes 14155780
  674.5 91.4 %all-to-all-start.2 = ((bf16[32,3,64,128]{3,2,1,0:T(8,128)(2,1)}), bf16[32,3,64,128]{3,2,1,0:T(8,128)(2,1)S(1)}, u32[]{:S(2)}, u32[]{:S(2)}) async-start(bf16[32,3,64,128]{3,2,1,0:T(8,128)(2,1)} %get-tuple-element.16), calls=%async_computation.2 | async-start | bytes 3145728 | tf_op jit(solution)/shard_map/all_to_all | solution.py:424
  765.9 1.2 copy-start.2
